TPU v7x, 32 devices: a whole 2x2x4 slice. The times are simulated.
32 devices in a mesh: island: 2 (over x), fsdp: 16 (over z, y, core).
Axes of the slice: x: 2, y: 2, z: 4, core: 2. Of those that a mesh axis runs over, the one named last changes fastest.
Arguments:
- partial_grads: bfloat16 [2, 16, 48, 28672], P('island', 'fsdp'), may hold values from -4 to 4, as said below
- inner_weights: bfloat16 [2, 48, 28672], P('island'), may hold values from -6 to 6
- outer_weights: float32 [48, 28672], P(None, 'fsdp'), may hold values from -6 to 6
- momentum: float32 [48, 28672], P(None, 'fsdp'), may hold values from -6 to 6
- round_draws: int32 [2, 48, 28672], P('island', None, 'fsdp'), may hold values from 0 to 255
- scale_exps: int32 [2, 48, 224], P('island', None, 'fsdp'), may hold values from -3 to 0
Outputs:
- new_outer: float32 [48, 28672], P(None, 'fsdp')
- new_momentum: float32 [48, 28672], P(None, 'fsdp')
- mixed_inner: bfloat16 [2, 48, 28672], P('island')
Inputs may be any that keep to these rules, and one draw needn't show every extreme that they name: `partial_grads`: every nonzero entry has magnitude 1/64 or more.
All inputs are finite; a program needn't handle non-finite values.
Results may differ from a plain program's by a relative error of at most 0.0054.
Values may be sent and summed in bfloat16 or wider, within the bound.
A program may use at most 64 MiB of HBM per device.

v0:
```python
import jax
import jax.numpy as jnp
from jax import lax
from jax.sharding import PartitionSpec as P

OUTER_RATE = 0.7
MOMENTUM_COEF = 0.9
MIX_WEIGHT = 0.5


def quantize(pseudo, round_draws, exponents):
    height = pseudo.shape[0]
    blocks = exponents.shape[-1]
    powers = jnp.left_shift(jnp.ones_like(exponents), exponents + 8).astype(jnp.float32) / 256.0
    scaled = pseudo.reshape(height, blocks, -1) / powers[..., None]
    dither = round_draws.reshape(height, blocks, -1).astype(jnp.float32) / 256.0
    levels = jnp.clip(jnp.floor(scaled + dither), -127.0, 127.0)
    return (levels * powers[..., None]).reshape(pseudo.shape)


def outer_update(average, outer_part, moment_part):
    moment_next = MOMENTUM_COEF * moment_part + average
    outer_next = outer_part - OUTER_RATE * (average + MOMENTUM_COEF * moment_next)
    return (outer_next, moment_next)


def blend_columns(inner_local, segment):
    return (
        MIX_WEIGHT * inner_local.astype(jnp.float32)
        + (1.0 - MIX_WEIGHT) * segment.astype(jnp.float32)
    ).astype(jnp.bfloat16)


def on_device(partial_grads, inner_weights, outer_weights, momentum, round_draws, scale_exps):
    local_terms = partial_grads[0, 0].astype(jnp.float32)
    pseudo = lax.psum_scatter(local_terms, "fsdp", scatter_dimension=1, tiled=True)
    dequant = quantize(pseudo, round_draws[0], scale_exps[0])
    island_count = lax.axis_size("island")
    inner_local = inner_weights[0]
    summed = lax.psum(dequant, "island")
    average = summed / island_count
    new_outer, new_momentum = outer_update(average, outer_weights, momentum)
    outer_half = new_outer.astype(jnp.bfloat16)
    mixed = blend_columns(inner_local, lax.all_gather(outer_half, "fsdp", axis=1, tiled=True))
    return (new_outer, new_momentum, mixed[None])


def solution(mesh):
    in_specs = (
        P("island", "fsdp", None, None),
        P("island", None, None),
        P(None, "fsdp"),
        P(None, "fsdp"),
        P("island", None, "fsdp"),
        P("island", None, "fsdp"),
    )
    out_specs = (P(None, "fsdp"), P(None, "fsdp"), P("island", None, None))
    return jax.shard_map(
        on_device, mesh=mesh, in_specs=in_specs, out_specs=out_specs, check_vma=False
    )
```

profile of v0, /device:TPU:1, one launch (start us, length us, event | category | flops | bytes accessed | tf_op | source)
XLA Modules:
  0.0 178.6 jit_solution(12433800789339548830)
XLA Ops:
  7.2 0.0 reduce-scatter.2.cloned.1.call-start
  7.2 4.6 %bitcast_convert_fusion = f32[48,28672]{1,0:T(8,128)} fusion(bf16[1,1,48,28672]{3,2,1,0:T(8,128)(2,1)} %param.6), kind=kLoop, calls=%fused_computation.4 | loop fusion | flops 1376256 | bytes 8257536 | tf_op jit(solution)/shard_map/convert_element_type | solution.py:35
  11.8 0.0 copy-start.3
  11.8 0.0 copy-start.1
  11.8 0.0 copy-start.2
  11.8 0.0 reduce-scatter.2.cloned.1.call-update
  11.8 0.0 copy-start
  11.8 0.0 all-reduce.2.cloned.1.call-start
  11.9 0.6 copy-done.3
  12.5 0.1 copy.11
  12.6 80.4 %reduce-scatter.2.cloned.1.call-done = f32[48,1792]{1,0:T(8,128)} async-done(((f32[48,28672]{1,0:T(8,128)}), f32[48,1792]{1,0:T(8,128)}) %reduce-scatter.2.cloned.1.call-update) | async-done | bytes 344080 | tf_op jit(solution)/shard_map/reduce_scatter | solution.py:36
  93.0 0.2 div.36
  93.2 0.0 copy-done.1
  93.2 1.9 %bitcast_multiply_fusion = f32[48,1792]{1,0:T(8,128)} fusion(f32[48,1792]{1,0:T(8,128)} %reduce-scatter.2.cloned.1.call-done, f32[6,8,14,128]{3,2,1,0:T(8,128)S(1)} %bitcast.23, s32[1,48,1792]{2,1,0:T(8,128)S(1)} %copy-done.1), kind=kLoop, calls=%fused_computation.5 | loop fusion | flops 602112 | bytes 1376256 | tf_op jit(solution)/shard_map/mul | solution.py:18
  95.1 0.0 all-reduce.2.cloned.1.call-update
  95.1 0.0 all-gather.2.cloned.1.call-start
  95.1 25.7 %all-reduce.2.cloned.1.call-done = f32[48,1792]{1,0:T(8,128)} async-done(((f32[48,1792]{1,0:T(8,128)}), f32[48,1792]{1,0:T(8,128)}) %all-reduce.2.cloned.1.call-update) | async-done | bytes 344080 | tf_op jit(solution)/shard_map/psum | solution.py:40
  120.9 0.0 copy-done.2
  120.9 2.1 %fusion.6 = (bf16[48,1792]{1,0:T(8,128)(2,1)}, f32[48,1792]{1,0:T(8,128)}, f32[48,1792]{1,0:T(8,128)}) fusion(f32[48,1792]{1,0:T(8,128)S(1)} %copy-done.2, f32[48,1792]{1,0:T(8,128)} %all-reduce.2.cloned.1.call-done, f32[48,1792]{1,0:T(8,128)} %param.9), kind=kLoop, calls=%fused_computation.13 | loop fusion | flops 688128 | bytes 1892352 | tf_op jit(solution)/shard_map/convert_element_type | solution.py:43
  123.0 0.0 all-gather.2.cloned.1.call-update
  123.0 45.0 %all-gather.2.cloned.1.call-done = bf16[48,28672]{1,0:T(8,128)(2,1)} async-done(((bf16[48,1792]{1,0:T(8,128)(2,1)}), bf16[48,28672]{1,0:T(8,128)(2,1)}) %all-gather.2.cloned.1.call-update) | async-done | bytes 2752528 | tf_op jit(solution)/shard_map/all_gather | solution.py:44
  168.0 0.0 copy-done
  168.0 4.1 %fusion.2 = bf16[1,48,28672]{2,1,0:T(8,128)(2,1)} fusion(bf16[48,28672]{1,0:T(8,128)(2,1)} %all-gather.2.cloned.1.call-done, bf16[1,48,28672]{2,1,0:T(8,128)(2,1)S(1)} %copy-done), kind=kLoop, calls=%fused_computation.3 | loop fusion | flops 6881280 | bytes 8257536 | tf_op jit(solution)/shard_map/broadcast_in_dim | solution.py:45
  (1 shorter events, 0.0 us)
Async XLA Ops:
  7.2 85.8 %reduce-scatter.2.cloned.1.call-start = ((), (), s32[]{:S(2)}) async-start(), calls=%async_computation.1 | async-start | bytes 5849088 | tf_op jit(solution)/shard_map/reduce_scatter | solution.py:36
  11.8 0.7 copy-start.3
  11.8 81.4 %copy-start.1 = (s32[1,48,1792]{2,1,0:T(8,128)S(1)}, s32[1,48,1792]{2,1,0:T(8,128)}, u32[]{:S(2)}) copy-start(s32[1,48,1792]{2,1,0:T(8,128)} %param.10) | copy-start | bytes 1032196
  11.8 109.1 %copy-start.2 = (f32[48,1792]{1,0:T(8,128)S(1)}, f32[48,1792]{1,0:T(8,128)}, u32[]{:S(2)}) copy-start(f32[48,1792]{1,0:T(8,128)} %param.8) | copy-start | bytes 1032196
  11.8 156.2 %copy-start = (bf16[1,48,28672]{2,1,0:T(8,128)(2,1)S(1)}, bf16[1,48,28672]{2,1,0:T(8,128)(2,1)}, u32[]{:S(2)}) copy-start(bf16[1,48,28672]{2,1,0:T(8,128)(2,1)} %param.7) | copy-start | bytes 8257540
  11.8 109.1 %all-reduce.2.cloned.1.call-start = ((), (), s32[]{:S(2)}) async-start(), calls=%async_computation.2 | async-start | bytes 688128 | tf_op jit(solution)/shard_map/psum | solution.py:40
  95.1 72.9 %all-gather.2.cloned.1.call-start = ((), (), s32[]{:S(2)}) async-start(), calls=%async_computation.3 | async-start | bytes 2924544 | tf_op jit(solution)/shard_map/all_gather | solution.py:44
Sparse Core Ops, SparseCore 0:
  11.9 81.0 reduce-scatter.1
  96.0 24.8 all-reduce.1
  123.9 44.0 all-gather.1
where the time goes:
time: 179 us
  waiting for transfers between devices  151 us (84%)
  between operations  13.8 us (8%)
  other arithmetic  12.7 us (7%)
    reduce_scatter x1, waiting for transfers between devices, on_device(): lax.psum_scatter(local_terms, 'fsdp', scatter_dimension=1, tiled=True)  80.4 us
    all_gather x1, waiting for transfers between devices, on_device(): lax.all_gather(outer_half, 'fsdp', axis=1, tiled=True)  45 us
    psum x1, waiting for transfers between devices, on_device(): summed = lax.psum(dequant, 'island')  25.7 us
    convert_element_type x1, other arithmetic, on_device(): local_terms = partial_grads[0, 0].astype(jnp.float32)  4.58 us
    broadcast_in_dim x1, other arithmetic, on_device(): return (new_outer, new_momentum, mixed[None])  4.11 us
  transfers between devices with their start and end apart: 3, of which 3 were waited for; matrix products, arithmetic and copies ran while one was open for 0% of the time, Pallas kernels for 0%

commit v1 on v0

v1 whole, which is shorter than its diff:
```python
import functools

import jax
import jax.numpy as jnp
from jax import lax
from jax.experimental import pallas as pl
from jax.experimental.pallas import tpu as pltpu
from jax.sharding import PartitionSpec as P

OUTER_RATE = 0.7
MOMENTUM_COEF = 0.9
MIX_WEIGHT = 0.5

MESH = pl.DeviceIdType.MESH
CHUNK = 16
LINE = 4
UNIT = 8192.0
LOW = 4


def remote(src, dst, send, recv, device):
    return pltpu.make_async_remote_copy(
        src_ref=src, dst_ref=dst, send_sem=send, recv_sem=recv,
        device_id=device, device_id_type=MESH,
    )


def kernel(A, B, I, W, R, grads, inner, outer, moment, draws, exps,
           new_outer, new_moment, mixed,
           mine, peer, sb, rb, sa, ra, acc, own_q, sx, rx, gat, blend,
           l1, s1, r1, s2, r2, s3, r3, s4, r4, s5, r5, s6, r6, s7, r7, inner_sem, out_sem):
    AB = A * B
    L = 128 * (-(-(W // 128) // 4))
    isl = lax.axis_index("island")
    f = lax.axis_index("fsdp")
    c = lax.rem(f, 2)
    ab = f // 2
    b = lax.rem(ab, B)
    a = ab // B
    core_dev = (isl, 2 * ab + 1 - c)

    def b_dev(k):
        return (isl, (a * B + lax.rem(b + k, B)) * 2 + c)

    def a_dev(k):
        return (isl, (lax.rem(a + k, A) * B + b) * 2 + c)

    def i_dev(k):
        return (lax.rem(isl + k, I), f)

    partners = ([core_dev] + [b_dev(k) for k in range(1, B)] + [a_dev(k) for k in range(1, A)]
                + [i_dev(k) for k in range(1, I)])

    def columns(block):
        return pl.ds(pl.multiple_of(block * W, 128), W)

    def rows(r):
        return pl.ds(r * CHUNK, CHUNK)

    inner_copy = pltpu.make_async_copy(inner, blend, inner_sem.at[0])
    inner_copy.start()
    for r in range(R):
        for j in range(AB):
            pltpu.make_async_copy(grads.at[rows(r), columns(2 * j + c)], mine.at[r, j], l1.at[r]).start()

    barrier = pltpu.get_barrier_semaphore()
    for device in partners:
        pl.semaphore_signal(barrier, inc=1, device_id=device, device_id_type=MESH)
    pl.semaphore_wait(barrier, len(partners))

    sends = []

    def begin(copy):
        copy.start()
        sends.append(copy)

    for r in range(R):
        for j in range(AB):
            remote(grads.at[rows(r), columns(2 * j + 1 - c)], peer.at[r, j], s1.at[r], r1.at[r], core_dev).start()

    def pair_sum(r, block):
        total = mine[r, block].astype(jnp.float32) + peer[r, block].astype(jnp.float32)
        return (total * UNIT).astype(jnp.int32)

    def stage1(r):
        pltpu.make_async_copy(mine.at[r], mine.at[r], l1.at[r]).wait()
        remote(peer.at[r], peer.at[r], s1.at[r], r1.at[r], core_dev).wait_recv()
        for k in range(1, B):
            target = lax.rem(b + k, B)
            low = None
            for j in range(A):
                s = pair_sum(r, j * B + target)
                sb[r, k - 1, j] = lax.shift_right_arithmetic(s, LOW).astype(jnp.int16)
                part = jnp.left_shift(jnp.bitwise_and(s, 15), LOW * j)
                low = part if low is None else low + part
            sb[r, k - 1, A] = low.astype(jnp.int16)
            begin(remote(sb.at[r, k - 1], rb.at[r, k - 1], s2.at[r, k - 1], r2.at[r, k - 1], b_dev(k)))

    def stage2(r):
        for k in range(1, B):
            remote(sb.at[r, k - 1], rb.at[r, k - 1], s2.at[r, k - 1], r2.at[r, k - 1], b_dev(k)).wait_recv()

        def column_sum(j):
            s = pair_sum(r, j * B + b)
            for k in range(1, B):
                high = jnp.left_shift(rb[r, k - 1, j].astype(jnp.int32), LOW)
                low = lax.shift_right_arithmetic(
                    rb[r, k - 1, A].astype(jnp.int32), jnp.full((CHUNK, W), LOW * j, jnp.int32))
                s = s + high + jnp.bitwise_and(low, 15)
            return s

        for k in range(1, A):
            s = column_sum(lax.rem(a + k, A))
            sa[r, k - 1, :, :W] = lax.shift_right_arithmetic(s, LOW).astype(jnp.int16)
            low = jnp.bitwise_and(s, 15)
            low = jnp.concatenate([low, jnp.zeros((CHUNK, 4 * L - W), jnp.int32)], axis=1) if 4 * L > W else low
            packed = low[:, :L]
            for q in range(1, 4):
                packed = packed + jnp.left_shift(low[:, q * L:(q + 1) * L], LOW * q)
            sa[r, k - 1, :, W:] = packed.astype(jnp.int16)
            begin(remote(sa.at[r, k - 1], ra.at[r, k - 1], s3.at[r, k - 1], r3.at[r, k - 1], a_dev(k)))
        acc[r] = column_sum(a)

    def powers(r, sign):
        e = exps[r * CHUNK:(r + 1) * CHUNK, :]
        p = jnp.left_shift(jnp.ones_like(e), 8 + sign * e).astype(jnp.float32) / 256.0
        return jnp.concatenate(
            [jnp.broadcast_to(p[:, t:t + 1], (CHUNK, 128)) for t in range(W // 128)], axis=1)

    def stage3(r):
        total = acc[r]
        for k in range(1, A):
            remote(sa.at[r, k - 1], ra.at[r, k - 1], s3.at[r, k - 1], r3.at[r, k - 1], a_dev(k)).wait_recv()
            high = jnp.left_shift(ra[r, k - 1, :, :W].astype(jnp.int32), LOW)
            packed = ra[r, k - 1, :, W:].astype(jnp.int32)
            low = jnp.concatenate(
                [jnp.bitwise_and(lax.shift_right_arithmetic(packed, jnp.full_like(packed, LOW * q)), 15)
                 for q in range(4)], axis=1)[:, :W]
            total = total + high + low
        pseudo = total.astype(jnp.float32) * (1.0 / UNIT)
        dither = draws[r * CHUNK:(r + 1) * CHUNK, :].astype(jnp.float32) * (1.0 / 256.0)
        levels = jnp.clip(jnp.floor(pseudo * powers(r, -1) + dither), -127.0, 127.0)
        dequant = levels * powers(r, 1)
        own_q[r] = dequant
        sx[r] = dequant.astype(jnp.bfloat16)
        for k in range(1, I):
            begin(remote(sx.at[r], rx.at[r, k - 1], s4.at[r, k - 1], r4.at[r, k - 1], i_dev(k)))

    def stage4(r):
        total = own_q[r]
        for k in range(1, I):
            remote(sx.at[r], rx.at[r, k - 1], s4.at[r, k - 1], r4.at[r, k - 1], i_dev(k)).wait_recv()
            total = total + rx[r, k - 1].astype(jnp.float32)
        average = total / I
        at = slice(r * CHUNK, (r + 1) * CHUNK)
        moment_next = MOMENTUM_COEF * moment[at, :] + average
        outer_next = outer[at, :] - OUTER_RATE * (average + MOMENTUM_COEF * moment_next)
        new_moment[at, :] = moment_next
        new_outer[at, :] = outer_next
        gat[r, c, b, a] = outer_next.astype(jnp.bfloat16)
        for k in range(1, A):
            begin(remote(gat.at[r, c, b, a], gat.at[r, c, b, a], s5.at[r, k - 1], r5.at[r, k - 1], a_dev(k)))

    def stage5(r):
        for k in range(1, A):
            came = gat.at[r, c, b, lax.rem(a + A - k, A)]
            remote(came, came, s5.at[r, k - 1], r5.at[r, k - 1], a_dev(k)).wait_recv()
        for k in range(1, B):
            begin(remote(gat.at[r, c, b], gat.at[r, c, b], s6.at[r, k - 1], r6.at[r, k - 1], b_dev(k)))

    def stage6(r):
        for k in range(1, B):
            came = gat.at[r, c, lax.rem(b + B - k, B)]
            remote(came, came, s6.at[r, k - 1], r6.at[r, k - 1], b_dev(k)).wait_recv()
        begin(remote(gat.at[r, c], gat.at[r, c], s7.at[r], r7.at[r], core_dev))

    def stage7(r):
        came = gat.at[r, 1 - c]
        remote(came, came, s7.at[r], r7.at[r], core_dev).wait_recv()
        if r == 0:
            inner_copy.wait()
        at = slice(r * CHUNK, (r + 1) * CHUNK)
        for core in range(2):
            for y in range(B):
                for z in range(A):
                    block = (z * B + y) * 2 + core
                    span = slice(block * W, (block + 1) * W)
                    value = MIX_WEIGHT * blend[at, span].astype(jnp.float32)
                    value = value + (1.0 - MIX_WEIGHT) * gat[r, core, y, z].astype(jnp.float32)
                    blend[at, span] = value.astype(jnp.bfloat16)
        pltpu.make_async_copy(blend.at[rows(r)], mixed.at[rows(r)], out_sem.at[r]).start()

    stages = [stage1, stage2, stage3, stage4, stage5, stage6, stage7]
    for t in range(R + len(stages) - 1):
        for index in range(len(stages)):
            r = t - index
            if 0 <= r < R:
                stages[index](r)

    for copy in sends:
        copy.wait_send()
    for r in range(R):
        remote(peer.at[r], peer.at[r], s1.at[r], r1.at[r], core_dev).wait_send()
        pltpu.make_async_copy(blend.at[rows(r)], mixed.at[rows(r)], out_sem.at[r]).wait()


def solution(mesh):
    I, n = mesh.shape["island"], mesh.shape["fsdp"]
    A = LINE
    B = n // (2 * A)

    def on_device(grads, inner, outer, moment, draws, exps):
        height, W = outer.shape
        R = height // CHUNK
        L = 128 * (-(-(W // 128) // 4))
        any_spec = pl.BlockSpec(memory_space=pl.ANY)
        vmem = pl.BlockSpec(memory_space=pltpu.VMEM)
        bf16, i16, f32, i32 = jnp.bfloat16, jnp.int16, jnp.float32, jnp.int32
        dma = pltpu.SemaphoreType.DMA
        bm, im = max(B - 1, 1), max(I - 1, 1)
        out = pl.pallas_call(
            functools.partial(kernel, A, B, I, W, R),
            out_shape=(
                jax.ShapeDtypeStruct(outer.shape, f32),
                jax.ShapeDtypeStruct(moment.shape, f32),
                jax.ShapeDtypeStruct(inner.shape[1:], bf16),
            ),
            in_specs=[any_spec, any_spec, vmem, vmem, vmem, vmem],
            out_specs=(vmem, vmem, any_spec),
            scratch_shapes=[
                pltpu.VMEM((R, A * B, CHUNK, W), bf16),
                pltpu.VMEM((R, A * B, CHUNK, W), bf16),
                pltpu.VMEM((R, bm, A + 1, CHUNK, W), i16),
                pltpu.VMEM((R, bm, A + 1, CHUNK, W), i16),
                pltpu.VMEM((R, A - 1, CHUNK, W + L), i16),
                pltpu.VMEM((R, A - 1, CHUNK, W + L), i16),
                pltpu.VMEM((R, CHUNK, W), i32),
                pltpu.VMEM((R, CHUNK, W), f32),
                pltpu.VMEM((R, CHUNK, W), bf16),
                pltpu.VMEM((R, im, CHUNK, W), bf16),
                pltpu.VMEM((R, 2, B, A, CHUNK, W), bf16),
                pltpu.VMEM(inner.shape[1:], bf16),
                dma((R,)), dma((R,)), dma((R,)),
                dma((R, bm)), dma((R, bm)),
                dma((R, A - 1)), dma((R, A - 1)),
                dma((R, im)), dma((R, im)),
                dma((R, A - 1)), dma((R, A - 1)),
                dma((R, bm)), dma((R, bm)),
                dma((R,)), dma((R,)),
                dma((1,)), dma((R,)),
            ],
            compiler_params=pltpu.CompilerParams(
                collective_id=0, has_side_effects=True, vmem_limit_bytes=48 * 1024 * 1024,
            ),
        )(grads[0, 0], inner[0], outer, moment, draws[0], exps[0])
        return out[0], out[1], out[2][None]

    in_specs = (
        P("island", "fsdp", None, None),
        P("island", None, None),
        P(None, "fsdp"),
        P(None, "fsdp"),
        P("island", None, "fsdp"),
        P("island", None, "fsdp"),
    )
    out_specs = (P(None, "fsdp"), P(None, "fsdp"), P("island", None, None))
    return jax.shard_map(
        on_device, mesh=mesh, in_specs=in_specs, out_specs=out_specs, check_vma=False
    )
```

time: 179 us -> 69.3 us (0.39)
  waiting for transfers between devices: 151 us -> 0 us
  Pallas kernels: 0 us -> 61 us
  between operations: 13.8 us -> 0.64 us
  other arithmetic: 12.7 us -> 0 us
  local copies, waits for them, and re-layouts: 0.86 us -> 6.71 us
    reduce_scatter x1 -> x0, waiting for transfers between devices: 80.4 us -> none  [on_device(): lax.psum_scatter(local_terms, 'fsdp', scatter_dimension=1, tiled=True)]
    pallas_call x0 -> x1, Pallas kernels: none -> 61 us  [on_device(): pl.pallas_call(functools.partial(kernel, A, B, I, W, R), out_shape=(jax.S...]
    all_gather x1 -> x0, waiting for transfers between devices: 45 us -> none  [on_device(): lax.all_gather(outer_half, 'fsdp', axis=1, tiled=True)]
    psum x1 -> x0, waiting for transfers between devices: 25.7 us -> none  [on_device(): summed = lax.psum(dequant, 'island')]
    convert_element_type x2 -> x0, other arithmetic: 6.65 us -> none  [the longest x1 4.58 us: on_device(): local_terms = partial_grads[0, 0].astype(jnp.float32)]
    unnamed x8 -> x10, local copies, waits for them, and re-layouts: 0.62 us -> 6.71 us
    broadcast_in_dim x1 -> x0, other arithmetic: 4.11 us -> none  [on_device(): return (new_outer, new_momentum, mixed[None])]
    mul x1 -> x0, other arithmetic: 1.9 us -> none  [quantize(): return (levels * powers[..., None]).reshape(pseudo.shape)]
  transfers between devices with their start and end apart: 3 -> 0, of which waited for: 3 -> 0; matrix products, arithmetic and copies ran while one was open for 0% -> 0% of each run, Pallas kernels for 0% -> 0%
where the time goes in v1:
time: 69.3 us; the launch traced here: 68.3 us
  Pallas kernels  61 us (88%)
  local copies, waits for them, and re-layouts  6.71 us (10%)
    pallas_call x1, Pallas kernels, on_device(): pl.pallas_call(functools.partial(kernel, A, B, I, W, R), out_shape=(jax.S...  61 us
    unnamed x10, local copies, waits for them, and re-layouts  6.71 us

profile of v1, /device:TPU:1, one launch (start us, length us, event | category | flops | bytes accessed | tf_op | source)
XLA Modules:
  0.0 68.3 jit_solution(9118979125534567003)
XLA Ops:
  0.6 0.8 %copy.9 = s32[1,48,14]{2,1,0:T(8,128)S(1)} copy(s32[1,48,14]{1,0,2:T(1,128)} %param.11) | data formatting | bytes 5376 | tf_op args[5]
  1.4 0.0 copy-start
  1.4 1.0 %copy-done = f32[48,1792]{1,0:T(8,128)S(1)} copy-done((f32[48,1792]{1,0:T(8,128)S(1)}, f32[48,1792]{1,0:T(8,128)}, u32[]{:S(2)}) %copy-start) | copy-done | bytes 344088
  2.4 0.0 copy-start.1
  2.4 1.0 %copy-done.1 = f32[48,1792]{1,0:T(8,128)S(1)} copy-done((f32[48,1792]{1,0:T(8,128)S(1)}, f32[48,1792]{1,0:T(8,128)}, u32[]{:S(2)}) %copy-start.1) | copy-done | bytes 344088
  3.4 0.0 copy-start.2
  3.4 1.0 %copy-done.2 = s32[1,48,1792]{2,1,0:T(8,128)S(1)} copy-done((s32[1,48,1792]{2,1,0:T(8,128)S(1)}, s32[1,48,1792]{2,1,0:T(8,128)}, u32[]{:S(2)}) %copy-start.2) | copy-done | bytes 344088
  4.3 61.0 %shard_map.85 = (f32[48,1792]{1,0:T(8,128)S(1)}, f32[48,1792]{1,0:T(8,128)S(1)}, bf16[48,28672]{1,0:T(8,128)(2,1)S(1)}) custom-call(bf16[48,28672]{1,0:T(8,128)(2,1)} %bitcast.8, bf16[48,28672]{1,0:T(8,128)(2,1)} %bitcast.9, f32[48,1792]{1,0:T(8,128)S(1)} %copy-done, f32[48,1792]{1,0:T(8,128)S(1)} %copy-done.1, s32[48,1792]{1,0:T(8,128)S(1)} %bitcast.6, ...), custom_call_target="tpu_custom_call" | custom-call | tf_op jit(solution)/shard_map/pallas_call | solution.py:221
  65.3 0.7 %copy.13 = f32[48,1792]{1,0:T(8,128)} copy(f32[48,1792]{1,0:T(8,128)S(1)} %get-tuple-element.12) | data formatting | bytes 688128
  66.1 0.7 %copy.14 = f32[48,1792]{1,0:T(8,128)} copy(f32[48,1792]{1,0:T(8,128)S(1)} %get-tuple-element.13) | data formatting | bytes 688128
  66.8 1.5 %copy.15 = bf16[1,48,28672]{2,1,0:T(8,128)(2,1)} copy(bf16[1,48,28672]{2,1,0:T(8,128)(2,1)S(1)} %bitcast.5) | data formatting | bytes 5505024
Async XLA Ops:
  1.4 1.0 %copy-start = (f32[48,1792]{1,0:T(8,128)S(1)}, f32[48,1792]{1,0:T(8,128)}, u32[]{:S(2)}) copy-start(f32[48,1792]{1,0:T(8,128)} %outer.1) | copy-start | bytes 1032196
  2.4 1.0 %copy-start.1 = (f32[48,1792]{1,0:T(8,128)S(1)}, f32[48,1792]{1,0:T(8,128)}, u32[]{:S(2)}) copy-start(f32[48,1792]{1,0:T(8,128)} %moment.1) | copy-start | bytes 1032196
  3.4 1.0 %copy-start.2 = (s32[1,48,1792]{2,1,0:T(8,128)S(1)}, s32[1,48,1792]{2,1,0:T(8,128)}, u32[]{:S(2)}) copy-start(s32[1,48,1792]{2,1,0:T(8,128)} %param.10) | copy-start | bytes 1032196

commit v2 on v1

v2 whole, which is shorter than its diff:
```python
import functools

import jax
import jax.numpy as jnp
from jax import lax
from jax.experimental import pallas as pl
from jax.experimental.pallas import tpu as pltpu
from jax.sharding import PartitionSpec as P

OUTER_RATE = 0.7
MOMENTUM_COEF = 0.9
MIX_WEIGHT = 0.5

MESH = pl.DeviceIdType.MESH
CHUNK = 16
LINE = 4
UNIT = 8192.0
PAIR_LOW = 2


def remote(src, dst, send, recv, device):
    return pltpu.make_async_remote_copy(
        src_ref=src, dst_ref=dst, send_sem=send, recv_sem=recv,
        device_id=device, device_id_type=MESH,
    )


def tiles_up(width, parts):
    return 128 * (-(-(width // 128) // parts))


def shift_right(value, amount):
    return lax.shift_right_arithmetic(value, jnp.full(value.shape, amount, jnp.int32))


def pack_low(value, bits, first, L):
    low = jnp.bitwise_and(value, 2 ** bits - 1)
    width = value.shape[1]
    packed = None
    for q in range(-(-width // L)):
        piece = low[:, q * L:(q + 1) * L]
        if piece.shape[1] < L:
            piece = jnp.concatenate([piece, jnp.zeros((value.shape[0], L - piece.shape[1]), jnp.int32)], axis=1)
        piece = jnp.left_shift(piece, bits * (first + q))
        packed = piece if packed is None else packed + piece
    return packed


def unpack(high, packed, bits, first, L):
    width = high.shape[1]
    low = [jnp.bitwise_and(shift_right(packed, bits * (first + q)), 2 ** bits - 1)
           for q in range(-(-width // L))]
    low = jnp.concatenate(low, axis=1)[:, :width]
    return jnp.left_shift(high.astype(jnp.int32), bits) + low


def kernel(A, B, I, W, R, grads, inner, outer_hbm, moment_hbm, draws_hbm, exps,
           new_outer, new_moment, mixed,
           mine, peer, sb, rb, sa, ra, acc, own_q, sx, rx, gat, blend, outer, moment, draws,
           l1, s1, r1, s2, r2, s3, r3, s4, r4, s5, r5, s6, r6, s7, r7, s8, r8, load_sem):
    AB = A * B
    PL = tiles_up(W, 2)
    ZB = (2 * B).bit_length()
    ZL = tiles_up(W, 16 // ZB)
    H = tiles_up(W, 2)
    isl = lax.axis_index("island")
    f = lax.axis_index("fsdp")
    h = lax.rem(isl, 2)
    c = lax.rem(f, 2)
    ab = f // 2
    b = lax.rem(ab, B)
    a = ab // B
    core_dev = (isl, 2 * ab + 1 - c)
    twin_dev = (isl + 1 - 2 * h, f)

    def b_dev(k):
        return (isl, (a * B + lax.rem(b + k, B)) * 2 + c)

    def a_dev(k):
        return (isl, (lax.rem(a + k, A) * B + b) * 2 + c)

    def i_dev(k):
        return (lax.rem(isl + k, I), f)

    partners = ([core_dev] + [b_dev(k) for k in range(1, B)] + [a_dev(k) for k in range(1, A)]
                + [i_dev(k) for k in range(1, I)])

    def columns(block):
        return pl.ds(pl.multiple_of(block * W, 128), W)

    def rows(r):
        return pl.ds(r * CHUNK, CHUNK)

    for r in range(R):
        for j in range(AB):
            pltpu.make_async_copy(grads.at[rows(r), columns(2 * j + c)], mine.at[r, j], l1.at[r]).start()

    barrier = pltpu.get_barrier_semaphore()
    for device in partners:
        pl.semaphore_signal(barrier, inc=1, device_id=device, device_id_type=MESH)
    pl.semaphore_wait(barrier, len(partners))

    sends = []

    def begin(copy):
        copy.start()
        sends.append(copy)

    for r in range(R):
        for j in range(AB):
            remote(grads.at[rows(r), columns(2 * j + 1 - c)], peer.at[r, j], s1.at[r], r1.at[r], core_dev).start()

    loads = [pltpu.make_async_copy(src, dst, load_sem.at[q]) for q, (src, dst) in enumerate(
        ((draws_hbm, draws), (outer_hbm, outer), (moment_hbm, moment), (inner, blend)))]
    for load in loads:
        load.start()

    def pair_sum(r, block):
        total = mine[r, block].astype(jnp.float32) + peer[r, block].astype(jnp.float32)
        return (total * UNIT).astype(jnp.int32)

    def stage1(r):
        pltpu.make_async_copy(mine.at[r], mine.at[r], l1.at[r]).wait()
        remote(peer.at[r], peer.at[r], s1.at[r], r1.at[r], core_dev).wait_recv()
        for k in range(1, B):
            target = lax.rem(b + k, B)
            low = None
            for j in range(A):
                s = pair_sum(r, j * B + target)
                sb[r, k - 1, :, j * W:(j + 1) * W] = shift_right(s, PAIR_LOW).astype(jnp.int16)
                part = pack_low(s, PAIR_LOW, 2 * j, PL)
                low = part if low is None else low + part
            sb[r, k - 1, :, A * W:] = low.astype(jnp.int16)
            begin(remote(sb.at[r, k - 1], rb.at[r, k - 1], s2.at[r, k - 1], r2.at[r, k - 1], b_dev(k)))

    def stage2(r):
        for k in range(1, B):
            remote(sb.at[r, k - 1], rb.at[r, k - 1], s2.at[r, k - 1], r2.at[r, k - 1], b_dev(k)).wait_recv()

        def column_sum(j):
            s = pair_sum(r, j * B + b)
            for k in range(1, B):
                s = s + unpack(rb[r, k - 1, :, columns(j)], rb[r, k - 1, :, A * W:].astype(jnp.int32),
                               PAIR_LOW, 2 * j, PL)
            return s

        for k in range(1, A):
            s = column_sum(lax.rem(a + k, A))
            sa[r, k - 1, :, :W] = shift_right(s, ZB).astype(jnp.int16)
            sa[r, k - 1, :, W:] = pack_low(s, ZB, 0, ZL).astype(jnp.int16)
            begin(remote(sa.at[r, k - 1], ra.at[r, k - 1], s3.at[r, k - 1], r3.at[r, k - 1], a_dev(k)))
        acc[r] = column_sum(a)

    def powers(r, sign):
        e = exps[r * CHUNK:(r + 1) * CHUNK, :]
        p = jnp.left_shift(jnp.ones_like(e), 8 + sign * e).astype(jnp.float32) / 256.0
        return jnp.concatenate(
            [jnp.broadcast_to(p[:, t:t + 1], (CHUNK, 128)) for t in range(W // 128)], axis=1)

    def stage3(r):
        if r == 0:
            loads[0].wait()
        total = acc[r]
        for k in range(1, A):
            remote(sa.at[r, k - 1], ra.at[r, k - 1], s3.at[r, k - 1], r3.at[r, k - 1], a_dev(k)).wait_recv()
            total = total + unpack(ra[r, k - 1, :, :W], ra[r, k - 1, :, W:].astype(jnp.int32), ZB, 0, ZL)
        pseudo = total.astype(jnp.float32) * (1.0 / UNIT)
        dither = draws[r * CHUNK:(r + 1) * CHUNK, :].astype(jnp.float32) * (1.0 / 256.0)
        levels = jnp.clip(jnp.floor(pseudo * powers(r, -1) + dither), -127.0, 127.0)
        dequant = levels * powers(r, 1)
        own_q[r] = dequant
        sx[r] = dequant.astype(jnp.bfloat16)
        for k in range(1, I):
            begin(remote(sx.at[r], rx.at[r, k - 1], s4.at[r, k - 1], r4.at[r, k - 1], i_dev(k)))

    def stage4(r):
        if r == 0:
            loads[1].wait()
            loads[2].wait()
        total = own_q[r]
        for k in range(1, I):
            remote(sx.at[r], rx.at[r, k - 1], s4.at[r, k - 1], r4.at[r, k - 1], i_dev(k)).wait_recv()
            total = total + rx[r, k - 1].astype(jnp.float32)
        average = total / I
        at = slice(r * CHUNK, (r + 1) * CHUNK)
        moment_next = MOMENTUM_COEF * moment[at, :] + average
        outer_next = outer[at, :] - OUTER_RATE * (average + MOMENTUM_COEF * moment_next)
        new_moment[at, :] = moment_next
        new_outer[at, :] = outer_next
        gat[r, h, c, b, a] = jnp.where(h == 0, outer_next[:, :H], outer_next[:, W - H:]).astype(jnp.bfloat16)
        for k in range(1, A):
            own = gat.at[r, h, c, b, a]
            begin(remote(own, own, s5.at[r, k - 1], r5.at[r, k - 1], a_dev(k)))

    def to_twin(r, k):
        part = gat.at[r, h, c, lax.rem(b + B - k, B)]
        return remote(part, part, s7.at[r, k], r7.at[r, k], twin_dev)

    def to_core(r, other, k):
        part = gat.at[r, 1 - h if other else h, c, lax.rem(b + B - k, B)]
        return remote(part, part, s8.at[r, other, k], r8.at[r, other, k], core_dev)

    def stage5(r):
        for k in range(1, A):
            came = gat.at[r, h, c, b, lax.rem(a + A - k, A)]
            remote(came, came, s5.at[r, k - 1], r5.at[r, k - 1], a_dev(k)).wait_recv()
        line = gat.at[r, h, c, b]
        for k in range(1, B):
            begin(remote(line, line, s6.at[r, k - 1], r6.at[r, k - 1], b_dev(k)))
        begin(to_twin(r, 0))
        begin(to_core(r, 0, 0))

    def stage6(r):
        for k in range(1, B):
            came = gat.at[r, h, c, lax.rem(b + B - k, B)]
            remote(came, came, s6.at[r, k - 1], r6.at[r, k - 1], b_dev(k)).wait_recv()
            begin(to_twin(r, k))
            begin(to_core(r, 0, k))

    def mix(r, core):
        at = slice(r * CHUNK, (r + 1) * CHUNK)
        for half in range(2):
            skip = half * (2 * H - W)
            for y in range(B):
                for z in range(A):
                    begin_at = ((z * B + y) * 2 + core) * W + half * H
                    span = pl.ds(pl.multiple_of(begin_at, 128), H - skip)
                    value = MIX_WEIGHT * blend[at, span].astype(jnp.float32)
                    segment = gat[r, half, core, y, z, :, skip:].astype(jnp.float32)
                    mixed[at, span] = (value + (1.0 - MIX_WEIGHT) * segment).astype(jnp.bfloat16)

    def stage7(r):
        for k in range(B):
            came = gat.at[r, 1 - h, c, lax.rem(b + B - k, B)]
            remote(came, came, s7.at[r, k], r7.at[r, k], twin_dev).wait_recv()
            begin(to_core(r, 1, k))
        if r == 0:
            loads[3].wait()
        mix(r, c)

    def stage8(r):
        for other in range(2):
            for k in range(B):
                came = gat.at[r, 1 - h if other else h, 1 - c, lax.rem(b + B - k, B)]
                remote(came, came, s8.at[r, other, k], r8.at[r, other, k], core_dev).wait_recv()
        mix(r, 1 - c)

    stages = [stage1, stage2, stage3, stage4, stage5, stage6, stage7, stage8]
    for t in range(R + len(stages) - 1):
        for index in range(len(stages)):
            r = t - index
            if 0 <= r < R:
                stages[index](r)

    for copy in sends:
        copy.wait_send()
    for r in range(R):
        remote(peer.at[r], peer.at[r], s1.at[r], r1.at[r], core_dev).wait_send()


def solution(mesh):
    I, n = mesh.shape["island"], mesh.shape["fsdp"]
    A = LINE
    B = n // (2 * A)

    def on_device(grads, inner, outer, moment, draws, exps):
        height, W = outer.shape
        R = height // CHUNK
        PL, H = tiles_up(W, 2), tiles_up(W, 2)
        ZL = tiles_up(W, 16 // (2 * B).bit_length())
        any_spec = pl.BlockSpec(memory_space=pl.ANY)
        vmem = pl.BlockSpec(memory_space=pltpu.VMEM)
        bf16, i16, f32, i32 = jnp.bfloat16, jnp.int16, jnp.float32, jnp.int32
        dma = pltpu.SemaphoreType.DMA
        bm, im = max(B - 1, 1), max(I - 1, 1)
        out = pl.pallas_call(
            functools.partial(kernel, A, B, I, W, R),
            out_shape=(
                jax.ShapeDtypeStruct(outer.shape, f32),
                jax.ShapeDtypeStruct(moment.shape, f32),
                jax.ShapeDtypeStruct(inner.shape[1:], bf16),
            ),
            in_specs=[any_spec, any_spec, any_spec, any_spec, any_spec, vmem],
            out_specs=(vmem, vmem, vmem),
            scratch_shapes=[
                pltpu.VMEM((R, A * B, CHUNK, W), bf16),
                pltpu.VMEM((R, A * B, CHUNK, W), bf16),
                pltpu.VMEM((R, bm, CHUNK, A * W + PL), i16),
                pltpu.VMEM((R, bm, CHUNK, A * W + PL), i16),
                pltpu.VMEM((R, A - 1, CHUNK, W + ZL), i16),
                pltpu.VMEM((R, A - 1, CHUNK, W + ZL), i16),
                pltpu.VMEM((R, CHUNK, W), i32),
                pltpu.VMEM((R, CHUNK, W), f32),
                pltpu.VMEM((R, CHUNK, W), bf16),
                pltpu.VMEM((R, im, CHUNK, W), bf16),
                pltpu.VMEM((R, 2, 2, B, A, CHUNK, H), bf16),
                pltpu.VMEM(inner.shape[1:], bf16),
                pltpu.VMEM(outer.shape, f32),
                pltpu.VMEM(outer.shape, f32),
                pltpu.VMEM(outer.shape, i32),
                dma((R,)), dma((R,)), dma((R,)),
                dma((R, bm)), dma((R, bm)),
                dma((R, A - 1)), dma((R, A - 1)),
                dma((R, im)), dma((R, im)),
                dma((R, A - 1)), dma((R, A - 1)),
                dma((R, bm)), dma((R, bm)),
                dma((R, B)), dma((R, B)),
                dma((R, 2, B)), dma((R, 2, B)),
                dma((4,)),
            ],
            compiler_params=pltpu.CompilerParams(
                collective_id=0, has_side_effects=True, vmem_limit_bytes=48 * 1024 * 1024,
            ),
        )(grads[0, 0], inner[0], outer, moment, draws[0], exps[0])
        return out[0], out[1], out[2][None]

    in_specs = (
        P("island", "fsdp", None, None),
        P("island", None, None),
        P(None, "fsdp"),
        P(None, "fsdp"),
        P("island", None, "fsdp"),
        P("island", None, "fsdp"),
    )
    out_specs = (P(None, "fsdp"), P(None, "fsdp"), P("island", None, None))
    return jax.shard_map(
        on_device, mesh=mesh, in_specs=in_specs, out_specs=out_specs, check_vma=False
    )
```

time: 69.3 us -> 64 us (0.924)
  Pallas kernels: 61 us -> 56.4 us
    pallas_call x1, Pallas kernels: 61 us -> 56.4 us  [on_device(): pl.pallas_call(functools.partial(kernel, A, B, I, W, R), out_shape=(jax.S...]
where the time goes in v2:
time: 64 us; the launch traced here: 63.7 us
  Pallas kernels  56.4 us (88%)
  local copies, waits for them, and re-layouts  6.71 us (10%)
  between operations  0.64 us (1%)
    pallas_call x1, Pallas kernels, on_device(): pl.pallas_call(functools.partial(kernel, A, B, I, W, R), out_shape=(jax.S...  56.4 us
    unnamed x10, local copies, waits for them, and re-layouts  6.71 us

profile of v2, /device:TPU:1, one launch (start us, length us, event | category | flops | bytes accessed | tf_op | source)
XLA Modules:
  0.0 63.7 jit_solution(1761481027738156148)
XLA Ops:
  0.6 0.8 %copy.9 = s32[1,48,14]{2,1,0:T(8,128)S(1)} copy(s32[1,48,14]{1,0,2:T(1,128)} %param.11) | data formatting | bytes 5376 | tf_op args[5]
  1.4 0.0 copy-start
  1.4 1.0 %copy-done = f32[48,1792]{1,0:T(8,128)S(1)} copy-done((f32[48,1792]{1,0:T(8,128)S(1)}, f32[48,1792]{1,0:T(8,128)}, u32[]{:S(2)}) %copy-start) | copy-done | bytes 344088
  2.4 0.0 copy-start.1
  2.4 1.0 %copy-done.1 = f32[48,1792]{1,0:T(8,128)S(1)} copy-done((f32[48,1792]{1,0:T(8,128)S(1)}, f32[48,1792]{1,0:T(8,128)}, u32[]{:S(2)}) %copy-start.1) | copy-done | bytes 344088
  3.4 0.0 copy-start.2
  3.4 1.0 %copy-done.2 = s32[1,48,1792]{2,1,0:T(8,128)S(1)} copy-done((s32[1,48,1792]{2,1,0:T(8,128)S(1)}, s32[1,48,1792]{2,1,0:T(8,128)}, u32[]{:S(2)}) %copy-start.2) | copy-done | bytes 344088
  4.3 56.4 %shard_map.85 = (f32[48,1792]{1,0:T(8,128)S(1)}, f32[48,1792]{1,0:T(8,128)S(1)}, bf16[48,28672]{1,0:T(8,128)(2,1)S(1)}) custom-call(bf16[48,28672]{1,0:T(8,128)(2,1)} %bitcast.8, bf16[48,28672]{1,0:T(8,128)(2,1)} %bitcast.9, f32[48,1792]{1,0:T(8,128)S(1)} %copy-done, f32[48,1792]{1,0:T(8,128)S(1)} %copy-done.1, s32[48,1792]{1,0:T(8,128)S(1)} %bitcast.6, ...), custom_call_target="tpu_custom_call" | custom-call | tf_op jit(solution)/shard_map/pallas_call | solution.py:276
  60.7 0.7 %copy.13 = f32[48,1792]{1,0:T(8,128)} copy(f32[48,1792]{1,0:T(8,128)S(1)} %get-tuple-element.12) | data formatting | bytes 688128
  61.4 0.7 %copy.14 = f32[48,1792]{1,0:T(8,128)} copy(f32[48,1792]{1,0:T(8,128)S(1)} %get-tuple-element.13) | data formatting | bytes 688128
  62.2 1.5 %copy.15 = bf16[1,48,28672]{2,1,0:T(8,128)(2,1)} copy(bf16[1,48,28672]{2,1,0:T(8,128)(2,1)S(1)} %bitcast.5) | data formatting | bytes 5505024
Async XLA Ops:
  1.4 1.0 %copy-start = (f32[48,1792]{1,0:T(8,128)S(1)}, f32[48,1792]{1,0:T(8,128)}, u32[]{:S(2)}) copy-start(f32[48,1792]{1,0:T(8,128)} %outer_hbm.1) | copy-start | bytes 1032196
  2.4 1.0 %copy-start.1 = (f32[48,1792]{1,0:T(8,128)S(1)}, f32[48,1792]{1,0:T(8,128)}, u32[]{:S(2)}) copy-start(f32[48,1792]{1,0:T(8,128)} %moment_hbm.1) | copy-start | bytes 1032196
  3.4 1.0 %copy-start.2 = (s32[1,48,1792]{2,1,0:T(8,128)S(1)}, s32[1,48,1792]{2,1,0:T(8,128)}, u32[]{:S(2)}) copy-start(s32[1,48,1792]{2,1,0:T(8,128)} %param.10) | copy-start | bytes 1032196

commit v3 on v2

v3 whole, which is shorter than its diff:
```python
import functools

import jax
import jax.numpy as jnp
from jax import lax
from jax.experimental import pallas as pl
from jax.experimental.pallas import tpu as pltpu
from jax.sharding import PartitionSpec as P

OUTER_RATE = 0.7
MOMENTUM_COEF = 0.9
MIX_WEIGHT = 0.5

MESH = pl.DeviceIdType.MESH
CHUNK = 16
LINE = 4
UNIT = 8192.0
PAIR_LOW = 2


def remote(src, dst, send, recv, device):
    return pltpu.make_async_remote_copy(
        src_ref=src, dst_ref=dst, send_sem=send, recv_sem=recv,
        device_id=device, device_id_type=MESH,
    )


def tiles_up(width, parts):
    return 128 * (-(-(width // 128) // parts))


def shift_right(value, amount):
    return lax.shift_right_arithmetic(value, jnp.full(value.shape, amount, jnp.int32))


def pack_low(value, bits, first, L):
    low = jnp.bitwise_and(value, 2 ** bits - 1)
    width = value.shape[1]
    packed = None
    for q in range(-(-width // L)):
        piece = low[:, q * L:(q + 1) * L]
        if piece.shape[1] < L:
            piece = jnp.concatenate([piece, jnp.zeros((value.shape[0], L - piece.shape[1]), jnp.int32)], axis=1)
        piece = jnp.left_shift(piece, bits * (first + q))
        packed = piece if packed is None else packed + piece
    return packed


def unpack(high, packed, bits, first, L):
    width = high.shape[1]
    low = [jnp.bitwise_and(shift_right(packed, bits * (first + q)), 2 ** bits - 1)
           for q in range(-(-width // L))]
    low = jnp.concatenate(low, axis=1)[:, :width]
    return jnp.left_shift(high.astype(jnp.int32), bits) + low


class Part:
    NAMES = (
        "mine", "peer", "sb", "rb", "sa", "ra", "acc", "own_q", "sx", "rx", "gat",
        "l1", "s1", "r1", "s2", "r2", "s3", "r3", "s4", "r4",
        "s5", "r5", "s6", "r6", "s7", "r7", "s8", "r8",
    )

    def __init__(self, offset, width, refs):
        self.offset, self.W = offset, width
        for name, ref in zip(self.NAMES, refs):
            setattr(self, name, ref)


def part_widths(width):
    first = 256 * (-(-(width // 128) // 4))
    return [first, width - first]


def kernel(A, B, I, WW, R, grads, inner, outer_hbm, moment_hbm, draws_hbm, exps,
           new_outer, new_moment, mixed, blend, outer, moment, draws, load_sem, *refs):
    AB = A * B
    ZB = (2 * B).bit_length()
    count = len(Part.NAMES)
    parts, offset = [], 0
    for p, width in enumerate(part_widths(WW)):
        parts.append(Part(offset, width, refs[p * count:(p + 1) * count]))
        offset += width
    chunks = [(r, part) for r in range(R) for part in parts]
    isl = lax.axis_index("island")
    f = lax.axis_index("fsdp")
    h = lax.rem(isl, 2)
    c = lax.rem(f, 2)
    ab = f // 2
    b = lax.rem(ab, B)
    a = ab // B
    core_dev = (isl, 2 * ab + 1 - c)
    twin_dev = (isl + 1 - 2 * h, f)

    def b_dev(k):
        return (isl, (a * B + lax.rem(b + k, B)) * 2 + c)

    def a_dev(k):
        return (isl, (lax.rem(a + k, A) * B + b) * 2 + c)

    def i_dev(k):
        return (lax.rem(isl + k, I), f)

    partners = ([core_dev] + [b_dev(k) for k in range(1, B)] + [a_dev(k) for k in range(1, A)]
                + [i_dev(k) for k in range(1, I)])

    def rows(r):
        return pl.ds(r * CHUNK, CHUNK)

    def source(r, g, block):
        return grads.at[rows(r), pl.ds(pl.multiple_of(block * WW + g.offset, 128), g.W)]

    def start_local(r, g):
        for j in range(AB):
            pltpu.make_async_copy(source(r, g, 2 * j + c), g.mine.at[r, j], g.l1.at[r]).start()

    def start_core(r, g):
        for j in range(AB):
            remote(source(r, g, 2 * j + 1 - c), g.peer.at[r, j], g.s1.at[r], g.r1.at[r], core_dev).start()

    ahead = 2
    for q in range(ahead):
        start_local(*chunks[q])

    barrier = pltpu.get_barrier_semaphore()
    for device in partners:
        pl.semaphore_signal(barrier, inc=1, device_id=device, device_id_type=MESH)
    pl.semaphore_wait(barrier, len(partners))

    sends = []

    def begin(copy):
        copy.start()
        sends.append(copy)

    for q in range(ahead):
        start_core(*chunks[q])

    loads = [pltpu.make_async_copy(src, dst, load_sem.at[q]) for q, (src, dst) in enumerate(
        ((draws_hbm, draws), (outer_hbm, outer), (moment_hbm, moment), (inner, blend)))]

    def pair_sum(r, g, block):
        total = g.mine[r, block].astype(jnp.float32) + g.peer[r, block].astype(jnp.float32)
        return (total * UNIT).astype(jnp.int32)

    def stage1(r, g):
        pltpu.make_async_copy(g.mine.at[r], g.mine.at[r], g.l1.at[r]).wait()
        remote(g.peer.at[r], g.peer.at[r], g.s1.at[r], g.r1.at[r], core_dev).wait_recv()
        for k in range(1, B):
            target = lax.rem(b + k, B)
            low = None
            for j in range(A):
                s = pair_sum(r, g, j * B + target)
                g.sb[r, k - 1, :, j * g.W:(j + 1) * g.W] = shift_right(s, PAIR_LOW).astype(jnp.int16)
                part = pack_low(s, PAIR_LOW, 2 * j, tiles_up(g.W, 2))
                low = part if low is None else low + part
            g.sb[r, k - 1, :, A * g.W:] = low.astype(jnp.int16)
            begin(remote(g.sb.at[r, k - 1], g.rb.at[r, k - 1], g.s2.at[r, k - 1], g.r2.at[r, k - 1], b_dev(k)))

    def stage2(r, g):
        for k in range(1, B):
            remote(g.sb.at[r, k - 1], g.rb.at[r, k - 1], g.s2.at[r, k - 1], g.r2.at[r, k - 1], b_dev(k)).wait_recv()

        def column_sum(j):
            s = pair_sum(r, g, j * B + b)
            for k in range(1, B):
                s = s + unpack(g.rb[r, k - 1, :, pl.ds(pl.multiple_of(j * g.W, 128), g.W)], g.rb[r, k - 1, :, A * g.W:].astype(jnp.int32),
                               PAIR_LOW, 2 * j, tiles_up(g.W, 2))
            return s

        for k in range(1, A):
            s = column_sum(lax.rem(a + k, A))
            g.sa[r, k - 1, :, :g.W] = shift_right(s, ZB).astype(jnp.int16)
            g.sa[r, k - 1, :, g.W:] = pack_low(s, ZB, 0, tiles_up(g.W, 16 // ZB)).astype(jnp.int16)
            begin(remote(g.sa.at[r, k - 1], g.ra.at[r, k - 1], g.s3.at[r, k - 1], g.r3.at[r, k - 1], a_dev(k)))
        g.acc[r] = column_sum(a)

    def powers(r, g, sign):
        e = exps[r * CHUNK:(r + 1) * CHUNK, :]
        p = jnp.left_shift(jnp.ones_like(e), 8 + sign * e).astype(jnp.float32) / 256.0
        return jnp.concatenate(
            [jnp.broadcast_to(p[:, t:t + 1], (CHUNK, 128))
             for t in range(g.offset // 128, (g.offset + g.W) // 128)], axis=1)

    def stage3(r, g):
        if r == 0 and g.offset == 0:
            loads[0].wait()
        total = g.acc[r]
        for k in range(1, A):
            remote(g.sa.at[r, k - 1], g.ra.at[r, k - 1], g.s3.at[r, k - 1], g.r3.at[r, k - 1], a_dev(k)).wait_recv()
            total = total + unpack(g.ra[r, k - 1, :, :g.W], g.ra[r, k - 1, :, g.W:].astype(jnp.int32), ZB, 0, tiles_up(g.W, 16 // ZB))
        pseudo = total.astype(jnp.float32) * (1.0 / UNIT)
        dither = draws[r * CHUNK:(r + 1) * CHUNK, g.offset:g.offset + g.W].astype(jnp.float32) * (1.0 / 256.0)
        levels = jnp.clip(jnp.floor(pseudo * powers(r, g, -1) + dither), -127.0, 127.0)
        dequant = levels * powers(r, g, 1)
        g.own_q[r] = dequant
        g.sx[r] = dequant.astype(jnp.bfloat16)
        for k in range(1, I):
            begin(remote(g.sx.at[r], g.rx.at[r, k - 1], g.s4.at[r, k - 1], g.r4.at[r, k - 1], i_dev(k)))

    def stage4(r, g):
        if r == 0 and g.offset == 0:
            loads[1].wait()
            loads[2].wait()
        total = g.own_q[r]
        for k in range(1, I):
            remote(g.sx.at[r], g.rx.at[r, k - 1], g.s4.at[r, k - 1], g.r4.at[r, k - 1], i_dev(k)).wait_recv()
            total = total + g.rx[r, k - 1].astype(jnp.float32)
        average = total / I
        at = (slice(r * CHUNK, (r + 1) * CHUNK), slice(g.offset, g.offset + g.W))
        H = tiles_up(g.W, 2)
        moment_next = MOMENTUM_COEF * moment[at] + average
        outer_next = outer[at] - OUTER_RATE * (average + MOMENTUM_COEF * moment_next)
        new_moment[at] = moment_next
        new_outer[at] = outer_next
        g.gat[r, h, c, b, a] = jnp.where(h == 0, outer_next[:, :H], outer_next[:, g.W - H:]).astype(jnp.bfloat16)
        for k in range(1, A):
            own = g.gat.at[r, h, c, b, a]
            begin(remote(own, own, g.s5.at[r, k - 1], g.r5.at[r, k - 1], a_dev(k)))

    def to_twin(r, g, k):
        part = g.gat.at[r, h, c, lax.rem(b + B - k, B)]
        return remote(part, part, g.s7.at[r, k], g.r7.at[r, k], twin_dev)

    def to_core(r, g, other, k):
        part = g.gat.at[r, 1 - h if other else h, c, lax.rem(b + B - k, B)]
        return remote(part, part, g.s8.at[r, other, k], g.r8.at[r, other, k], core_dev)

    def stage5(r, g):
        for k in range(1, A):
            came = g.gat.at[r, h, c, b, lax.rem(a + A - k, A)]
            remote(came, came, g.s5.at[r, k - 1], g.r5.at[r, k - 1], a_dev(k)).wait_recv()
        line = g.gat.at[r, h, c, b]
        for k in range(1, B):
            begin(remote(line, line, g.s6.at[r, k - 1], g.r6.at[r, k - 1], b_dev(k)))
        begin(to_twin(r, g, 0))
        begin(to_core(r, g, 0, 0))

    def stage6(r, g):
        for k in range(1, B):
            came = g.gat.at[r, h, c, lax.rem(b + B - k, B)]
            remote(came, came, g.s6.at[r, k - 1], g.r6.at[r, k - 1], b_dev(k)).wait_recv()
            begin(to_twin(r, g, k))
            begin(to_core(r, g, 0, k))

    def mix(r, g, core):
        H = tiles_up(g.W, 2)
        at = slice(r * CHUNK, (r + 1) * CHUNK)
        for half in range(2):
            skip = half * (2 * H - g.W)
            for y in range(B):
                for z in range(A):
                    begin_at = ((z * B + y) * 2 + core) * WW + g.offset + half * H
                    span = pl.ds(pl.multiple_of(begin_at, 128), H - skip)
                    value = MIX_WEIGHT * blend[at, span].astype(jnp.float32)
                    segment = g.gat[r, half, core, y, z, :, skip:].astype(jnp.float32)
                    mixed[at, span] = (value + (1.0 - MIX_WEIGHT) * segment).astype(jnp.bfloat16)

    def stage7(r, g):
        for k in range(B):
            came = g.gat.at[r, 1 - h, c, lax.rem(b + B - k, B)]
            remote(came, came, g.s7.at[r, k], g.r7.at[r, k], twin_dev).wait_recv()
            begin(to_core(r, g, 1, k))
        if r == 0 and g.offset == 0:
            loads[3].wait()
        mix(r, g, c)

    def stage8(r, g):
        for other in range(2):
            for k in range(B):
                came = g.gat.at[r, 1 - h if other else h, 1 - c, lax.rem(b + B - k, B)]
                remote(came, came, g.s8.at[r, other, k], g.r8.at[r, other, k], core_dev).wait_recv()
        mix(r, g, 1 - c)

    stages = [stage1, stage2, stage3, stage4, stage5, stage6, stage7, stage8]
    lags = [0, 2, 4, 5, 6, 7, 8, 9]
    for t in range(len(chunks) + lags[-1]):
        for stage, lag in zip(stages, lags):
            if 0 <= t - lag < len(chunks):
                stage(*chunks[t - lag])
            if lag == 0 and t + ahead < len(chunks):
                start_local(*chunks[t + ahead])
                start_core(*chunks[t + ahead])
        if t == 1:
            for load in loads:
                load.start()

    for copy in sends:
        copy.wait_send()
    for r, g in chunks:
        remote(g.peer.at[r], g.peer.at[r], g.s1.at[r], g.r1.at[r], core_dev).wait_send()


def part_scratch(A, B, I, W, R):
    bf16, i16, f32, i32 = jnp.bfloat16, jnp.int16, jnp.float32, jnp.int32
    dma = pltpu.SemaphoreType.DMA
    bm, im = max(B - 1, 1), max(I - 1, 1)
    PL, ZL = tiles_up(W, 2), tiles_up(W, 16 // (2 * B).bit_length())
    return [
        pltpu.VMEM((R, A * B, CHUNK, W), bf16),
        pltpu.VMEM((R, A * B, CHUNK, W), bf16),
        pltpu.VMEM((R, bm, CHUNK, A * W + PL), i16),
        pltpu.VMEM((R, bm, CHUNK, A * W + PL), i16),
        pltpu.VMEM((R, A - 1, CHUNK, W + ZL), i16),
        pltpu.VMEM((R, A - 1, CHUNK, W + ZL), i16),
        pltpu.VMEM((R, CHUNK, W), i32),
        pltpu.VMEM((R, CHUNK, W), f32),
        pltpu.VMEM((R, CHUNK, W), bf16),
        pltpu.VMEM((R, im, CHUNK, W), bf16),
        pltpu.VMEM((R, 2, 2, B, A, CHUNK, PL), bf16),
        dma((R,)), dma((R,)), dma((R,)),
        dma((R, bm)), dma((R, bm)),
        dma((R, A - 1)), dma((R, A - 1)),
        dma((R, im)), dma((R, im)),
        dma((R, A - 1)), dma((R, A - 1)),
        dma((R, bm)), dma((R, bm)),
        dma((R, B)), dma((R, B)),
        dma((R, 2, B)), dma((R, 2, B)),
    ]


def solution(mesh):
    I, n = mesh.shape["island"], mesh.shape["fsdp"]
    A = LINE
    B = n // (2 * A)

    def on_device(grads, inner, outer, moment, draws, exps):
        height, W = outer.shape
        R = height // CHUNK
        any_spec = pl.BlockSpec(memory_space=pl.ANY)
        vmem = pl.BlockSpec(memory_space=pltpu.VMEM)
        bf16, i16, f32, i32 = jnp.bfloat16, jnp.int16, jnp.float32, jnp.int32
        dma = pltpu.SemaphoreType.DMA
        out = pl.pallas_call(
            functools.partial(kernel, A, B, I, W, R),
            out_shape=(
                jax.ShapeDtypeStruct(outer.shape, f32),
                jax.ShapeDtypeStruct(moment.shape, f32),
                jax.ShapeDtypeStruct(inner.shape[1:], bf16),
            ),
            in_specs=[any_spec, any_spec, any_spec, any_spec, any_spec, vmem],
            out_specs=(vmem, vmem, vmem),
            scratch_shapes=[
                pltpu.VMEM(inner.shape[1:], bf16),
                pltpu.VMEM(outer.shape, f32),
                pltpu.VMEM(outer.shape, f32),
                pltpu.VMEM(outer.shape, i32),
                dma((4,)),
            ] + [shape for width in part_widths(W) for shape in part_scratch(A, B, I, width, R)],
            compiler_params=pltpu.CompilerParams(
                collective_id=0, has_side_effects=True, vmem_limit_bytes=48 * 1024 * 1024,
            ),
        )(grads[0, 0], inner[0], outer, moment, draws[0], exps[0])
        return out[0], out[1], out[2][None]

    in_specs = (
        P("island", "fsdp", None, None),
        P("island", None, None),
        P(None, "fsdp"),
        P(None, "fsdp"),
        P("island", None, "fsdp"),
        P("island", None, "fsdp"),
    )
    out_specs = (P(None, "fsdp"), P(None, "fsdp"), P("island", None, None))
    return jax.shard_map(
        on_device, mesh=mesh, in_specs=in_specs, out_specs=out_specs, check_vma=False
    )
```

time: 64 us -> 62.9 us (0.983)
  Pallas kernels: 56.4 us -> 55.1 us
    pallas_call x1, Pallas kernels: 56.4 us -> 55.1 us  [on_device(): pl.pallas_call(functools.partial(kernel, A, B, I, W, R), out_shape=(jax.S...]
where the time goes in v3:
time: 62.9 us; the launch traced here: 62.5 us
  Pallas kernels  55.1 us (88%)
  local copies, waits for them, and re-layouts  6.71 us (11%)
  between operations  0.64 us (1%)
    pallas_call x1, Pallas kernels, on_device(): pl.pallas_call(functools.partial(kernel, A, B, I, W, R), out_shape=(jax.S...  55.1 us
    unnamed x10, local copies, waits for them, and re-layouts  6.71 us

profile of v3, /device:TPU:1, one launch (start us, length us, event | category | flops | bytes accessed | tf_op | source)
XLA Modules:
  0.0 62.5 jit_solution(11281046221297032568)
XLA Ops:
  0.6 0.8 %copy.9 = s32[1,48,14]{2,1,0:T(8,128)S(1)} copy(s32[1,48,14]{1,0,2:T(1,128)} %param.11) | data formatting | bytes 5376 | tf_op args[5]
  1.4 0.0 copy-start
  1.4 1.0 %copy-done = f32[48,1792]{1,0:T(8,128)S(1)} copy-done((f32[48,1792]{1,0:T(8,128)S(1)}, f32[48,1792]{1,0:T(8,128)}, u32[]{:S(2)}) %copy-start) | copy-done | bytes 344088
  2.4 0.0 copy-start.1
  2.4 1.0 %copy-done.1 = f32[48,1792]{1,0:T(8,128)S(1)} copy-done((f32[48,1792]{1,0:T(8,128)S(1)}, f32[48,1792]{1,0:T(8,128)}, u32[]{:S(2)}) %copy-start.1) | copy-done | bytes 344088
  3.4 0.0 copy-start.2
  3.4 1.0 %copy-done.2 = s32[1,48,1792]{2,1,0:T(8,128)S(1)} copy-done((s32[1,48,1792]{2,1,0:T(8,128)S(1)}, s32[1,48,1792]{2,1,0:T(8,128)}, u32[]{:S(2)}) %copy-start.2) | copy-done | bytes 344088
  4.3 55.1 %shard_map.85 = (f32[48,1792]{1,0:T(8,128)S(1)}, f32[48,1792]{1,0:T(8,128)S(1)}, bf16[48,28672]{1,0:T(8,128)(2,1)S(1)}) custom-call(bf16[48,28672]{1,0:T(8,128)(2,1)} %bitcast.8, bf16[48,28672]{1,0:T(8,128)(2,1)} %bitcast.9, f32[48,1792]{1,0:T(8,128)S(1)} %copy-done, f32[48,1792]{1,0:T(8,128)S(1)} %copy-done.1, s32[48,1792]{1,0:T(8,128)S(1)} %bitcast.6, ...), custom_call_target="tpu_custom_call" | custom-call | tf_op jit(solution)/shard_map/pallas_call | solution.py:334
  59.5 0.7 %copy.13 = f32[48,1792]{1,0:T(8,128)} copy(f32[48,1792]{1,0:T(8,128)S(1)} %get-tuple-element.12) | data formatting | bytes 688128
  60.2 0.7 %copy.14 = f32[48,1792]{1,0:T(8,128)} copy(f32[48,1792]{1,0:T(8,128)S(1)} %get-tuple-element.13) | data formatting | bytes 688128
  60.9 1.5 %copy.15 = bf16[1,48,28672]{2,1,0:T(8,128)(2,1)} copy(bf16[1,48,28672]{2,1,0:T(8,128)(2,1)S(1)} %bitcast.5) | data formatting | bytes 5505024
Async XLA Ops:
  1.4 1.0 %copy-start = (f32[48,1792]{1,0:T(8,128)S(1)}, f32[48,1792]{1,0:T(8,128)}, u32[]{:S(2)}) copy-start(f32[48,1792]{1,0:T(8,128)} %outer_hbm.1) | copy-start | bytes 1032196
  2.4 1.0 %copy-start.1 = (f32[48,1792]{1,0:T(8,128)S(1)}, f32[48,1792]{1,0:T(8,128)}, u32[]{:S(2)}) copy-start(f32[48,1792]{1,0:T(8,128)} %moment_hbm.1) | copy-start | bytes 1032196
  3.4 1.0 %copy-start.2 = (s32[1,48,1792]{2,1,0:T(8,128)S(1)}, s32[1,48,1792]{2,1,0:T(8,128)}, u32[]{:S(2)}) copy-start(s32[1,48,1792]{2,1,0:T(8,128)} %param.10) | copy-start | bytes 1032196

commit v4 on v3

--- a/solution.py
+++ b/solution.py
@@ -273,7 +273,7 @@
         mix(r, g, 1 - c)
 
     stages = [stage1, stage2, stage3, stage4, stage5, stage6, stage7, stage8]
-    lags = [0, 2, 4, 5, 6, 7, 8, 9]
+    lags = [0, 1, 2, 3, 4, 5, 6, 7]
     for t in range(len(chunks) + lags[-1]):
         for stage, lag in zip(stages, lags):
             if 0 <= t - lag < len(chunks):

time: 62.9 us -> 61.2 us (0.973)
  Pallas kernels: 55.1 us -> 53.5 us
    pallas_call x1, Pallas kernels: 55.1 us -> 53.5 us  [on_device(): pl.pallas_call(functools.partial(kernel, A, B, I, W, R), out_shape=(jax.S...]
where the time goes in v4:
time: 61.2 us; the launch traced here: 60.9 us
  Pallas kernels  53.5 us (87%)
  local copies, waits for them, and re-layouts  6.71 us (11%)
  between operations  0.64 us (1%)
    pallas_call x1, Pallas kernels, on_device(): pl.pallas_call(functools.partial(kernel, A, B, I, W, R), out_shape=(jax.S...  53.5 us
    unnamed x10, local copies, waits for them, and re-layouts  6.71 us

profile of v4, /device:TPU:1, one launch (start us, length us, event | category | flops | bytes accessed | tf_op | source)
XLA Modules:
  0.0 60.9 jit_solution(2316672062065558874)
XLA Ops:
  0.6 0.8 %copy.9 = s32[1,48,14]{2,1,0:T(8,128)S(1)} copy(s32[1,48,14]{1,0,2:T(1,128)} %param.11) | data formatting | bytes 5376 | tf_op args[5]
  1.4 0.0 copy-start
  1.4 1.0 %copy-done = f32[48,1792]{1,0:T(8,128)S(1)} copy-done((f32[48,1792]{1,0:T(8,128)S(1)}, f32[48,1792]{1,0:T(8,128)}, u32[]{:S(2)}) %copy-start) | copy-done | bytes 344088
  2.4 0.0 copy-start.1
  2.4 1.0 %copy-done.1 = f32[48,1792]{1,0:T(8,128)S(1)} copy-done((f32[48,1792]{1,0:T(8,128)S(1)}, f32[48,1792]{1,0:T(8,128)}, u32[]{:S(2)}) %copy-start.1) | copy-done | bytes 344088
  3.4 0.0 copy-start.2
  3.4 1.0 %copy-done.2 = s32[1,48,1792]{2,1,0:T(8,128)S(1)} copy-done((s32[1,48,1792]{2,1,0:T(8,128)S(1)}, s32[1,48,1792]{2,1,0:T(8,128)}, u32[]{:S(2)}) %copy-start.2) | copy-done | bytes 344088
  4.3 53.5 %shard_map.85 = (f32[48,1792]{1,0:T(8,128)S(1)}, f32[48,1792]{1,0:T(8,128)S(1)}, bf16[48,28672]{1,0:T(8,128)(2,1)S(1)}) custom-call(bf16[48,28672]{1,0:T(8,128)(2,1)} %bitcast.8, bf16[48,28672]{1,0:T(8,128)(2,1)} %bitcast.9, f32[48,1792]{1,0:T(8,128)S(1)} %copy-done, f32[48,1792]{1,0:T(8,128)S(1)} %copy-done.1, s32[48,1792]{1,0:T(8,128)S(1)} %bitcast.6, ...), custom_call_target="tpu_custom_call" | custom-call | tf_op jit(solution)/shard_map/pallas_call | solution.py:334
  57.9 0.7 %copy.13 = f32[48,1792]{1,0:T(8,128)} copy(f32[48,1792]{1,0:T(8,128)S(1)} %get-tuple-element.12) | data formatting | bytes 688128
  58.6 0.7 %copy.14 = f32[48,1792]{1,0:T(8,128)} copy(f32[48,1792]{1,0:T(8,128)S(1)} %get-tuple-element.13) | data formatting | bytes 688128
  59.4 1.5 %copy.15 = bf16[1,48,28672]{2,1,0:T(8,128)(2,1)} copy(bf16[1,48,28672]{2,1,0:T(8,128)(2,1)S(1)} %bitcast.5) | data formatting | bytes 5505024
Async XLA Ops:
  1.4 1.0 %copy-start = (f32[48,1792]{1,0:T(8,128)S(1)}, f32[48,1792]{1,0:T(8,128)}, u32[]{:S(2)}) copy-start(f32[48,1792]{1,0:T(8,128)} %outer_hbm.1) | copy-start | bytes 1032196
  2.4 1.0 %copy-start.1 = (f32[48,1792]{1,0:T(8,128)S(1)}, f32[48,1792]{1,0:T(8,128)}, u32[]{:S(2)}) copy-start(f32[48,1792]{1,0:T(8,128)} %moment_hbm.1) | copy-start | bytes 1032196
  3.4 1.0 %copy-start.2 = (s32[1,48,1792]{2,1,0:T(8,128)S(1)}, s32[1,48,1792]{2,1,0:T(8,128)}, u32[]{:S(2)}) copy-start(s32[1,48,1792]{2,1,0:T(8,128)} %param.10) | copy-start | bytes 1032196
